TPU v7x, 512 devices: a whole 4x4x16 slice. The times are simulated.
512 devices in a mesh: row: 16 (over z), col: 16 (over y_hi, x, core), chan: 2 (over y_lo).
Axes of the slice: x: 4, y: 4 (y_hi: 2, y_lo: 2; y = y_hi * 2 + y_lo), z: 16, core: 2. Of those that a mesh axis runs over, the one named last changes fastest.
Arguments:
- array_volts: bfloat16 [6, 2, 2048, 2048], P('chan', None, ('row', 'col')), parts along dimension 0, may hold values from -15 to 15, as said below
- reference_volts: bfloat16 [6, 2, 32, 2048], P('chan', None, None, 'col'), parts along dimension 0, may hold values from -15 to 15, as said below
Outputs:
- cleaned: float32 [6, 2, 2048, 2048], P('chan', None, 'row', 'col'), parts along dimension 0
There are 2 independent parts, one for each index of `chan`. A program takes and returns all parts, laid end to end along the dimension named above; each array names one. Nothing has to cross between parts.
Inputs may be any that keep to these rules, and one draw needn't show every extreme that they name: `array_volts`: array voltages: common interference from a few sources plus independent noise. `reference_volts`: reference voltages: the same interference sources seen with other gains, plus independent noise.
All inputs are finite; a program needn't handle non-finite values.
Results may differ from a plain program's by a relative error of at most 0.0003.
Values may be sent and summed in bfloat16 or wider, within the bound.
A program may use at most 64 MiB of HBM per device.

v0:
```python
import jax
import jax.numpy as jnp
from jax import lax
from jax.sharding import PartitionSpec as P


def in_order(blocks, dim):
    shape = list(blocks.shape[1:])
    shape[dim] *= blocks.shape[0]
    return jnp.moveaxis(blocks, 0, dim).reshape(shape)


def sent_to_all(x, axis):
    copies = jnp.broadcast_to(x, (lax.axis_size(axis), *x.shape))
    return lax.all_to_all(copies, axis, split_axis=0, concat_axis=0, tiled=True)


def collect(x, axis, dim):
    return in_order(sent_to_all(x, axis), dim)


def correlate(first_rows, second_rows):
    width_first = first_rows.shape[1]
    width_second = second_rows.shape[1]
    samples = first_rows.shape[2]
    stacked_first = first_rows.reshape(2 * width_first, samples)
    stacked_second = second_rows.reshape(2 * width_second, samples)
    product = jnp.einsum(
        "xn,yn->xy", stacked_first, stacked_second, preferred_element_type=jnp.float32
    )
    real_part = product[:width_first, :width_second] + product[width_first:, width_second:]
    imaginary_portion = product[width_first:, :width_second] - product[:width_first, width_second:]
    return jnp.stack([real_part, imaginary_portion]) / jnp.float32(samples)


def subtract(vis_tile, rows_cross, cross_cols, reference_covariance):
    real_cov = reference_covariance[0]
    imag_cov = reference_covariance[1]
    system = jnp.concatenate(
        [jnp.concatenate([real_cov, -imag_cov], 1), jnp.concatenate([imag_cov, real_cov], 1)], 0
    )
    lower_factor = jnp.linalg.cholesky(system)
    right_hand = jnp.concatenate([cross_cols[0], cross_cols[1]], 0)
    middle = lax.linalg.triangular_solve(lower_factor, right_hand, left_side=True, lower=True)
    solved = lax.linalg.triangular_solve(
        lower_factor, middle, left_side=True, lower=True, transpose_a=True
    )
    half_size = real_cov.shape[0]
    solved_real = solved[:half_size]
    solved_imag = solved[half_size:]
    highest = lax.Precision.HIGHEST
    corr_real = jnp.dot(rows_cross[0], solved_real, precision=highest) - jnp.dot(
        rows_cross[1], solved_imag, precision=highest
    )
    corr_imag = jnp.dot(rows_cross[0], solved_imag, precision=highest) + jnp.dot(
        rows_cross[1], solved_real, precision=highest
    )
    return vis_tile - jnp.stack([corr_real, corr_imag])


def per_device(array_volts, reference_volts):
    results = []
    for sub_index in range(array_volts.shape[0]):
        local_volts = array_volts[sub_index]
        ref_all = collect(reference_volts[sub_index], "col", 2)
        reference_covariance = correlate(ref_all, ref_all)
        row_volts = collect(local_volts, "col", 1)
        width_rows = row_volts.shape[1]
        left_factor_matrix = jnp.concatenate([row_volts, ref_all], 1)
        joined = correlate(
            left_factor_matrix, lax.all_gather(local_volts, "row", axis=1, tiled=True)
        )
        vis_tile = joined[:, :width_rows]
        cross_cols = joined[:, width_rows:]
        rows_cross = correlate(row_volts, ref_all)
        results.append(subtract(vis_tile, rows_cross, cross_cols, reference_covariance))
    return jnp.stack(results)


def solution(mesh):
    return jax.shard_map(
        per_device,
        mesh=mesh,
        in_specs=(P("chan", None, ("row", "col"), None), P("chan", None, None, "col")),
        out_specs=P("chan", None, "row", "col"),
        check_vma=False,
    )
```

profile of v0, /device:TPU:6, one launch (start us, length us, event | category | flops | bytes accessed | tf_op | source)
XLA Modules:
  0.0 237.5 jit_solution(3841975494435622801)
XLA Ops:
  6.5 1.6 fusion.99
  8.2 0.7 all-gather.9.cloned.1.call-update
  8.9 0.8 slice_bitcast_fusion.20
  9.7 0.8 broadcast_in_dim.24
  10.4 9.2 %all-to-all-start.5 = ((bf16[16,2,32,128]{3,2,1,0:T(8,128)(2,1)}), bf16[16,2,32,128]{3,2,1,0:T(8,128)(2,1)S(1)}, u32[]{:S(2)}, u32[]{:S(2)}) async-start(bf16[16,2,32,128]{3,2,1,0:T(8,128)(2,1)} %broadcast_in_dim.24), calls=%async_computation.5 | async-start | bytes 524288 | tf_op jit(solution)/shard_map/all_to_all | solution.py:15
  19.7 0.7 all-gather.7.cloned.1.call-update
  20.4 6.3 %all-to-all-done.5 = bf16[16,2,32,128]{3,2,1,0:T(8,128)(2,1)S(1)} async-done(((bf16[16,2,32,128]{3,2,1,0:T(8,128)(2,1)}), bf16[16,2,32,128]{3,2,1,0:T(8,128)(2,1)S(1)}, u32[]{:S(2)}, u32[]{:S(2)}) %all-to-all-start.5) | async-done | bytes 262176 | tf_op jit(solution)/shard_map/all_to_all | solution.py:15
  26.7 0.8 broadcast_in_dim.22
  27.5 5.8 %all-to-all-start.3 = ((bf16[16,2,32,128]{3,2,1,0:T(8,128)(2,1)}), bf16[16,2,32,128]{3,2,1,0:T(8,128)(2,1)S(1)}, u32[]{:S(2)}, u32[]{:S(2)}) async-start(bf16[16,2,32,128]{3,2,1,0:T(8,128)(2,1)} %broadcast_in_dim.22), calls=%async_computation.3 | async-start | bytes 524288 | tf_op jit(solution)/shard_map/all_to_all | solution.py:15
  34.1 6.2 %all-to-all-done.3 = bf16[16,2,32,128]{3,2,1,0:T(8,128)(2,1)S(1)} async-done(((bf16[16,2,32,128]{3,2,1,0:T(8,128)(2,1)}), bf16[16,2,32,128]{3,2,1,0:T(8,128)(2,1)S(1)}, u32[]{:S(2)}, u32[]{:S(2)}) %all-to-all-start.3) | async-done | bytes 262176 | tf_op jit(solution)/shard_map/all_to_all | solution.py:15
  40.3 0.8 broadcast_in_dim.20
  41.1 5.8 %all-to-all-start.1 = ((bf16[16,2,32,128]{3,2,1,0:T(8,128)(2,1)}), bf16[16,2,32,128]{3,2,1,0:T(8,128)(2,1)S(1)}, u32[]{:S(2)}, u32[]{:S(2)}) async-start(bf16[16,2,32,128]{3,2,1,0:T(8,128)(2,1)} %broadcast_in_dim.20), calls=%async_computation.1 | async-start | bytes 524288 | tf_op jit(solution)/shard_map/all_to_all | solution.py:15
  47.8 6.2 %all-to-all-done.1 = bf16[16,2,32,128]{3,2,1,0:T(8,128)(2,1)S(1)} async-done(((bf16[16,2,32,128]{3,2,1,0:T(8,128)(2,1)}), bf16[16,2,32,128]{3,2,1,0:T(8,128)(2,1)S(1)}, u32[]{:S(2)}, u32[]{:S(2)}) %all-to-all-start.1) | async-done | bytes 262176 | tf_op jit(solution)/shard_map/all_to_all | solution.py:15
  54.0 1.1 broadcast_in_dim.23
  55.1 5.9 %all-to-all-start.4 = ((bf16[16,2,8,2048]{3,2,1,0:T(8,128)(2,1)}), bf16[16,2,8,2048]{3,2,1,0:T(8,128)(2,1)S(1)}, u32[]{:S(2)}, u32[]{:S(2)}) async-start(bf16[16,2,8,2048]{3,2,1,0:T(8,128)(2,1)} %broadcast_in_dim.23), calls=%async_computation.4 | async-start | bytes 2097152 | tf_op jit(solution)/shard_map/all_to_all | solution.py:15
  61.2 0.7 copy-done.6
  62.5 5.9 %cholesky.81 = f32[64,64]{1,0:T(8,128)S(1)} custom-call(f32[64,64]{1,0:T(8,128)S(1)} %fusion.51), custom_call_target="Cholesky" | custom-call | tf_op jit(solution)/shard_map/jit(cholesky)/cholesky | solution.py:42
  68.4 0.7 compare_reduce_fusion
  69.3 5.9 %cholesky.70 = f32[64,64]{1,0:T(8,128)S(1)} custom-call(f32[64,64]{1,0:T(8,128)S(1)} %fusion.55), custom_call_target="Cholesky" | custom-call | tf_op jit(solution)/shard_map/jit(cholesky)/cholesky | solution.py:42
  75.4 5.9 %cholesky.59 = f32[64,64]{1,0:T(8,128)S(1)} custom-call(f32[64,64]{1,0:T(8,128)S(1)} %fusion.59), custom_call_target="Cholesky" | custom-call | tf_op jit(solution)/shard_map/jit(cholesky)/cholesky | solution.py:42
  81.3 0.7 compare_reduce_fusion.1
  82.0 0.6 fusion.35
  82.7 0.6 fusion.34
  83.4 1.1 broadcast_in_dim.21
  84.5 7.3 %all-to-all-start.2 = ((bf16[16,2,8,2048]{3,2,1,0:T(8,128)(2,1)}), bf16[16,2,8,2048]{3,2,1,0:T(8,128)(2,1)S(1)}, u32[]{:S(2)}, u32[]{:S(2)}) async-start(bf16[16,2,8,2048]{3,2,1,0:T(8,128)(2,1)} %broadcast_in_dim.21), calls=%async_computation.2 | async-start | bytes 2097152 | tf_op jit(solution)/shard_map/all_to_all | solution.py:15
  91.7 0.7 compare_reduce_fusion.2
  92.4 0.7 copy_bitcast_fusion.1
  93.1 0.7 copy_bitcast_fusion.2
  93.8 12.6 %all-to-all-done.2 = bf16[16,2,8,2048]{3,2,1,0:T(8,128)(2,1)S(1)} async-done(((bf16[16,2,8,2048]{3,2,1,0:T(8,128)(2,1)}), bf16[16,2,8,2048]{3,2,1,0:T(8,128)(2,1)S(1)}, u32[]{:S(2)}, u32[]{:S(2)}) %all-to-all-start.2) | async-done | bytes 1048608 | tf_op jit(solution)/shard_map/all_to_all | solution.py:15
  106.4 1.1 broadcast_in_dim.19
  107.5 7.5 %all-to-all-start = ((bf16[16,2,8,2048]{3,2,1,0:T(8,128)(2,1)}), bf16[16,2,8,2048]{3,2,1,0:T(8,128)(2,1)}, u32[]{:S(2)}, u32[]{:S(2)}) async-start(bf16[16,2,8,2048]{3,2,1,0:T(8,128)(2,1)} %broadcast_in_dim.19), calls=%async_computation | async-start | bytes 2097152 | tf_op jit(solution)/shard_map/all_to_all | solution.py:15
  115.0 0.6 fusion.33
  115.7 4.9 %custom-call.17 = f32[1,64,64]{1,2,0:T(8,128)S(1)} custom-call(f32[1,64,64]{2,1,0:T(8,128)S(1)} %fusion.35), custom_call_target="InvertDiagBlocksLowerTriangular" | custom-call | tf_op jit(solution)/shard_map/triangular_solve/custom-call.2 | solution.py:45
  120.6 4.9 %custom-call.15 = f32[1,64,64]{1,2,0:T(8,128)S(1)} custom-call(f32[1,64,64]{2,1,0:T(8,128)S(1)} %fusion.34), custom_call_target="InvertDiagBlocksLowerTriangular" | custom-call | tf_op jit(solution)/shard_map/triangular_solve/custom-call.2 | solution.py:45
  125.5 4.9 %custom-call.13 = f32[1,64,64]{1,2,0:T(8,128)S(1)} custom-call(f32[1,64,64]{2,1,0:T(8,128)S(1)} %fusion.33), custom_call_target="InvertDiagBlocksLowerTriangular" | custom-call | tf_op jit(solution)/shard_map/triangular_solve/custom-call.2 | solution.py:45
  130.6 0.8 copy-done.3
  131.5 0.4 fusion.8
  131.9 0.4 fusion.12
  132.4 1.3 copy.120
  133.8 0.4 fusion.16
  134.2 1.2 pad_maximum_fusion.2
  135.6 0.8 copy-done
  136.5 2.2 fusion.102
  138.7 16.8 %all-gather.9.cloned.1.call-done = bf16[1,2,128,2048]{3,2,1,0:T(8,128)(2,1)} async-done(((bf16[1,2,8,2048]{3,2,1,0:T(8,128)(2,1)}), bf16[1,2,128,2048]{3,2,1,0:T(8,128)(2,1)}) %all-gather.9.cloned.1.call-update) | async-done | bytes 1048592 | tf_op jit(solution)/shard_map/all_gather | solution.py:71
  155.5 1.8 fusion.101
  159.4 66.2 %all-gather.7.cloned.1.call-done = bf16[1,2,128,2048]{3,2,1,0:T(8,128)(2,1)} async-done(((bf16[1,2,8,2048]{3,2,1,0:T(8,128)(2,1)}), bf16[1,2,128,2048]{3,2,1,0:T(8,128)(2,1)}) %all-gather.7.cloned.1.call-update) | async-done | bytes 1048592 | tf_op jit(solution)/shard_map/all_gather | solution.py:71
  225.6 1.8 fusion.100
  230.2 0.8 pad_maximum_fusion.3
  (90 shorter events, 8.4 us)
Async XLA Ops:
  6.5 130.0 %all-gather.11.cloned.1.call-start = ((), (), s32[]{:S(2)}) async-start(), calls=%async_computation.8 | async-start | bytes 1114112 | tf_op jit(solution)/shard_map/all_gather | solution.py:71
  8.2 147.4 %all-gather.9.cloned.1.call-start = ((), (), s32[]{:S(2)}) async-start(), calls=%async_computation.7 | async-start | bytes 1114112 | tf_op jit(solution)/shard_map/all_gather | solution.py:71
  10.4 16.3 %all-to-all-start.5 = ((bf16[16,2,32,128]{3,2,1,0:T(8,128)(2,1)}), bf16[16,2,32,128]{3,2,1,0:T(8,128)(2,1)S(1)}, u32[]{:S(2)}, u32[]{:S(2)}) async-start(bf16[16,2,32,128]{3,2,1,0:T(8,128)(2,1)} %broadcast_in_dim.24), calls=%async_computation.5 | async-start | bytes 524288 | tf_op jit(solution)/shard_map/all_to_all | solution.py:15
  19.6 205.9 %all-gather.7.cloned.1.call-start = ((), (), s32[]{:S(2)}) async-start(), calls=%async_computation.6 | async-start | bytes 1114112 | tf_op jit(solution)/shard_map/all_gather | solution.py:71
  27.5 12.9 %all-to-all-start.3 = ((bf16[16,2,32,128]{3,2,1,0:T(8,128)(2,1)}), bf16[16,2,32,128]{3,2,1,0:T(8,128)(2,1)S(1)}, u32[]{:S(2)}, u32[]{:S(2)}) async-start(bf16[16,2,32,128]{3,2,1,0:T(8,128)(2,1)} %broadcast_in_dim.22), calls=%async_computation.3 | async-start | bytes 524288 | tf_op jit(solution)/shard_map/all_to_all | solution.py:15
  33.4 0.7 copy-start.2
  41.1 12.9 %all-to-all-start.1 = ((bf16[16,2,32,128]{3,2,1,0:T(8,128)(2,1)}), bf16[16,2,32,128]{3,2,1,0:T(8,128)(2,1)S(1)}, u32[]{:S(2)}, u32[]{:S(2)}) async-start(bf16[16,2,32,128]{3,2,1,0:T(8,128)(2,1)} %broadcast_in_dim.20), calls=%async_computation.1 | async-start | bytes 524288 | tf_op jit(solution)/shard_map/all_to_all | solution.py:15
  47.1 0.7 copy-start.4
  55.1 28.3 %all-to-all-start.4 = ((bf16[16,2,8,2048]{3,2,1,0:T(8,128)(2,1)}), bf16[16,2,8,2048]{3,2,1,0:T(8,128)(2,1)S(1)}, u32[]{:S(2)}, u32[]{:S(2)}) async-start(bf16[16,2,8,2048]{3,2,1,0:T(8,128)(2,1)} %broadcast_in_dim.23), calls=%async_computation.4 | async-start | bytes 2097152 | tf_op jit(solution)/shard_map/all_to_all | solution.py:15
  61.2 0.7 copy-start.6
  84.5 22.0 %all-to-all-start.2 = ((bf16[16,2,8,2048]{3,2,1,0:T(8,128)(2,1)}), bf16[16,2,8,2048]{3,2,1,0:T(8,128)(2,1)S(1)}, u32[]{:S(2)}, u32[]{:S(2)}) async-start(bf16[16,2,8,2048]{3,2,1,0:T(8,128)(2,1)} %broadcast_in_dim.21), calls=%async_computation.2 | async-start | bytes 2097152 | tf_op jit(solution)/shard_map/all_to_all | solution.py:15
  107.5 24.9 %all-to-all-start = ((bf16[16,2,8,2048]{3,2,1,0:T(8,128)(2,1)}), bf16[16,2,8,2048]{3,2,1,0:T(8,128)(2,1)}, u32[]{:S(2)}, u32[]{:S(2)}) async-start(bf16[16,2,8,2048]{3,2,1,0:T(8,128)(2,1)} %broadcast_in_dim.19), calls=%async_computation | async-start | bytes 2097152 | tf_op jit(solution)/shard_map/all_to_all | solution.py:15
  130.5 1.0 copy-start.3
  130.5 1.4 copy-start.5
  132.4 1.4 copy-start.7
  134.2 1.2 copy-start.1
  135.4 1.0 copy-start
Sparse Core Ops, SparseCore 0:
  9.4 75.5 all-gather.10
  87.2 68.3 all-gather.8
  157.6 67.8 all-gather.6
where the time goes:
time: 239 us; the launch traced here: 238 us
  waiting for transfers between devices  116 us (49%)
  starting transfers between devices  41.5 us (17%)
  other arithmetic  39.4 us (16%)
  local copies, waits for them, and re-layouts  14.8 us (6%)
  between operations  13.7 us (6%)
  matrix products  12.3 us (5%)
    all_gather x3, waiting for transfers between devices, per_device(): lax.all_gather(local_volts, 'row', axis=1, tiled=True)  83 us
    all_to_all x6, starting transfers between devices, sent_to_all(): return lax.all_to_all(copies, axis, split_axis=0, concat_axis=0, tiled=True)  41.5 us
    all_to_all x6, waiting for transfers between devices, sent_to_all(): return lax.all_to_all(copies, axis, split_axis=0, concat_axis=0, tiled=True)  31.3 us
    another operation x9, other arithmetic, subtract(): lower_factor = jnp.linalg.cholesky(system)  19.7 us
    another operation x6, other arithmetic, subtract(): lax.linalg.triangular_solve(lower_factor, middle, left_side=True, lower=T...  16.6 us
    dot_general x9, matrix products, correlate(): jnp.einsum('xn,yn->xy', stacked_first, stacked_second, preferred_element_...  7.68 us
    broadcast_in_dim x6, local copies, waits for them, and re-layouts, sent_to_all(): copies = jnp.broadcast_to(x, (lax.axis_size(axis), *x.shape))  5.59 us
  transfers between devices with their start and end apart: 9, of which 6 were waited for; matrix products, arithmetic and copies ran while one was open for 24% of the time, Pallas kernels for 0%

commit v1 on v0

v1 whole, which is shorter than its diff:
```python
import functools

import jax
import jax.numpy as jnp
from jax import lax
from jax.experimental import pallas as pl
from jax.experimental.pallas import tpu as pltpu
from jax.sharding import PartitionSpec as P

MESH = pl.DeviceIdType.MESH
F32, BF16 = jnp.float32, jnp.bfloat16
SUBS, NREF, ANTS, SAMPLES = 3, 32, 8, 2048
ROWS, COLS, NX = 16, 16, 4
PAIR = 2 * ANTS
LANES = 512

FROM_Y, LEFT, RIGHT, LEFT_Y, RIGHT_Y, LEFT_2, RIGHT_2, OWN = range(8)


def kernel(volts, refs, out, colb, rowb, refb, ref_all, ref_mix, hi, lo, inv, *sems):
    z_send, z_recv, g_send, g_recv, c_send, c_recv = sems
    row, col = lax.axis_index("row"), lax.axis_index("col")
    up, down = lax.rem(row + 1, ROWS), lax.rem(row + ROWS - 1, ROWS)
    y, x, core = col // (2 * NX), lax.rem(col // 2, NX), lax.rem(col, 2)

    def at(dy, dx, other=False):
        yy = 1 - y if dy else y
        cc = 1 - core if other else core
        return yy * (2 * NX) + lax.rem(x + dx + NX, NX) * 2 + cc

    origin = {
        FROM_Y: at(1, 0), LEFT: at(0, -1), RIGHT: at(0, 1), LEFT_Y: at(1, -1),
        RIGHT_Y: at(1, 1), LEFT_2: at(0, 2), RIGHT_2: at(1, 2), OWN: col,
    }
    to_y, to_left, to_right, to_core = at(1, 0), at(0, -1), at(0, 1), at(0, 0, True)

    barrier = pltpu.get_barrier_semaphore()
    for axis, there in (
        ("row", up), ("row", down), ("col", to_y), ("col", to_left), ("col", to_right), ("col", to_core),
    ):
        pl.semaphore_signal(barrier, inc=1, device_id={axis: there}, device_id_type=MESH)
    pl.semaphore_wait(barrier, 6)

    def hops(way, sub):
        return 8 if (sub % 2) == way else 7

    def z_copy(way, hop, sub):
        start = lax.rem(row + (ROWS - hop if way == 0 else hop), ROWS)
        place = colb.at[sub, start]
        return pltpu.make_async_remote_copy(
            src_ref=volts.at[sub] if hop == 0 else place,
            dst_ref=place,
            send_sem=z_send.at[way, hop, sub],
            recv_sem=z_recv.at[way, hop, sub],
            device_id={"row": up if way == 0 else down},
            device_id_type=MESH,
        )

    def z_step(hop, sub):
        for way in range(2):
            if hop < hops(way, sub):
                z_copy(way, hop, sub).wait_recv()
                if hop + 1 < hops(way, sub):
                    z_copy(way, hop + 1, sub).start()

    def z_sent(hop):
        for way in range(2):
            for sub in range(SUBS):
                if hop < hops(way, sub):
                    z_copy(way, hop, sub).wait_send()

    def shard(kind, slot):
        return refb.at[slot] if kind == 0 else rowb.at[:, slot]

    def g_copy(kind, received, slot, there):
        mine = refs if kind == 0 else volts
        return pltpu.make_async_remote_copy(
            src_ref=mine if received in (FROM_Y, LEFT, RIGHT) else shard(kind, slot),
            dst_ref=shard(kind, slot),
            send_sem=g_send.at[kind, received],
            recv_sem=g_recv.at[kind, received],
            device_id={"col": there},
            device_id_type=MESH,
        )

    def g_send_copy(kind, received):
        slot, there = {
            FROM_Y: (col, to_y), LEFT: (col, to_right), RIGHT: (col, to_left),
            LEFT_Y: (origin[FROM_Y], to_right), RIGHT_Y: (origin[FROM_Y], to_left),
            LEFT_2: (origin[LEFT], to_right), RIGHT_2: (origin[RIGHT_Y], to_left),
        }[received]
        return g_copy(kind, received, slot, there)

    def core_copy(kind, received):
        slot = origin[received]
        mine = refs if kind == 0 else volts
        return pltpu.make_async_remote_copy(
            src_ref=mine if received == OWN else shard(kind, slot),
            dst_ref=shard(kind, slot),
            send_sem=c_send.at[kind, received],
            recv_sem=c_recv.at[kind, received],
            device_id={"col": to_core},
            device_id_type=MESH,
        )

    def g_start(kind):
        for received in (FROM_Y, LEFT, RIGHT):
            g_send_copy(kind, received).start()
        core_copy(kind, OWN).start()

    def g_arrived(kind, *those):
        for received in those:
            g_copy(kind, received, origin[received], to_left).wait_recv()
            core_copy(kind, received).start()

    def g_forward(kind, *those):
        for received in those:
            g_send_copy(kind, received).start()

    def core_arrived(kind):
        for received in range(8):
            core_copy(kind, received).wait_recv()

    def g_sent(kind):
        for received in range(7):
            g_send_copy(kind, received).wait_send()
        for received in range(8):
            core_copy(kind, received).wait_send()

    def gather_references():
        for sub in range(SUBS):
            whole = jnp.concatenate([refb[c, sub] for c in range(COLS)], axis=1)
            ref_all[sub] = whole
            real, imag = whole[:NREF], whole[NREF:]
            one = jnp.concatenate([real, -imag], axis=0)
            two = jnp.concatenate([imag, real], axis=0)
            ref_mix[sub, 0] = jnp.concatenate([one, one, one], axis=0)
            ref_mix[sub, 1] = jnp.concatenate([two, two, two], axis=0)

    def product(a, b):
        return lax.dot_general(a, b, (((1,), (1,)), ((), ())), preferred_element_type=F32)

    def covariance():
        for sub in range(SUBS):
            g = product(ref_all[sub], ref_all[sub])
            inv[0, sub] = g[:NREF, :NREF] + g[NREF:, NREF:]
            inv[1, sub] = g[NREF:, :NREF] - g[:NREF, NREF:]

    def eliminate(first, last):
        lane = lax.broadcasted_iota(jnp.int32, (SUBS, NREF, NREF), 2)
        line = lax.broadcasted_iota(jnp.int32, (SUBS, NREF, NREF), 1)

        def step(k, carry):
            re, im = carry
            on_lane, on_line = lane == k, line == k
            col_re = jnp.sum(jnp.where(on_lane, re, 0.0), axis=2, keepdims=True)
            col_im = jnp.sum(jnp.where(on_lane, im, 0.0), axis=2, keepdims=True)
            row_re = jnp.sum(jnp.where(on_line, re, 0.0), axis=1, keepdims=True)
            row_im = jnp.sum(jnp.where(on_line, im, 0.0), axis=1, keepdims=True)
            both = jnp.logical_and(on_lane, on_line)
            pivot = jnp.sum(
                jnp.sum(jnp.where(both, re, 0.0), axis=2, keepdims=True), axis=1, keepdims=True
            )
            scale = 1.0 / pivot
            first_lane = lax.broadcasted_iota(jnp.int32, (SUBS, 1, NREF), 2) == k
            row_re = jnp.where(first_lane, 1.0, row_re) * scale
            row_im = jnp.where(first_lane, 0.0, row_im) * scale
            new_re = jnp.where(on_lane, 0.0, re) - (col_re * row_re - col_im * row_im)
            new_im = jnp.where(on_lane, 0.0, im) - (col_re * row_im + col_im * row_re)
            return jnp.where(on_line, row_re, new_re), jnp.where(on_line, row_im, new_im)

        re, im = lax.fori_loop(first, last, step, (inv[0], inv[1]))
        inv[0] = re
        inv[1] = im

    def weights(sub):
        q = product(rowb[sub].reshape(COLS * PAIR, SAMPLES), ref_all[sub])
        q = q.reshape(COLS, 2, ANTS, 2 * NREF)
        cross_re = (q[:, 0, :, :NREF] + q[:, 1, :, NREF:]).reshape(COLS * ANTS, NREF)
        cross_im = (q[:, 1, :, :NREF] - q[:, 0, :, NREF:]).reshape(COLS * ANTS, NREF)
        re, im = inv[0, sub], inv[1, sub]
        cross = jnp.concatenate([cross_re, cross_im], axis=1)
        system = jnp.concatenate(
            [jnp.concatenate([re, im], axis=1), jnp.concatenate([-im, re], axis=1)], axis=0
        )
        w = jnp.dot(cross, system, precision=lax.Precision.HIGHEST, preferred_element_type=F32)
        w1 = w.astype(BF16)
        rest = w - w1.astype(F32)
        w2 = rest.astype(BF16)
        w3 = (rest - w2.astype(F32)).astype(BF16)
        return jnp.concatenate([w1, w2, w3], axis=1)

    def clean_rows(sub, w, part):
        here = pl.ds(part * LANES, LANES)
        raw = rowb[sub, :, :, here].astype(F32).reshape(COLS, 2, ANTS, LANES)
        for p in range(2):
            one = raw[:, p].reshape(COLS * ANTS, LANES)
            one = one - jnp.dot(w, ref_mix[sub, p, :, here], preferred_element_type=F32)
            top = one.astype(BF16)
            hi[sub, pl.ds(p * 128, 128), here] = top
            lo[sub, pl.ds(p * 128, 128), here] = (one - top.astype(F32)).astype(BF16)

    def finish(sub):
        b = colb[sub].reshape(ROWS * PAIR, SAMPLES)
        t = product(b, hi[sub]) + product(b, lo[sub])
        t = t.reshape(ROWS, 2, ANTS, 256)
        re = (t[:, 0, :, :128] + t[:, 1, :, 128:]).reshape(ROWS * ANTS, 128)
        im = (t[:, 0, :, 128:] - t[:, 1, :, :128]).reshape(ROWS * ANTS, 128)
        out[sub, 0] = re.T * (1.0 / SAMPLES)
        out[sub, 1] = im.T * (1.0 / SAMPLES)

    for sub in range(SUBS):
        for way in range(2):
            z_copy(way, 0, sub).start()
        if sub == 0:
            g_start(0)
    g_start(1)
    for sub in range(SUBS):
        colb[sub, row] = volts[sub]
        rowb[sub, col] = volts[sub]
    refb[col] = refs[...]

    z_step(0, 0)
    g_arrived(0, FROM_Y, LEFT, RIGHT)
    g_forward(0, LEFT_Y, RIGHT_Y, LEFT_2)
    z_step(0, 1)
    z_step(0, 2)
    g_arrived(0, LEFT_Y, RIGHT_Y, LEFT_2)
    g_forward(0, RIGHT_2)
    z_step(1, 0)
    g_arrived(1, FROM_Y, LEFT, RIGHT)
    g_forward(1, LEFT_Y, RIGHT_Y, LEFT_2)
    g_arrived(0, RIGHT_2)
    z_step(1, 1)
    z_step(1, 2)
    core_arrived(0)
    gather_references()
    z_step(2, 0)
    covariance()
    z_step(2, 1)
    eliminate(0, 6)
    z_step(2, 2)
    g_arrived(1, LEFT_Y, RIGHT_Y)
    g_forward(1, RIGHT_2)
    eliminate(6, 12)
    for sub in range(SUBS):
        z_step(3, sub)
        eliminate(12 + 6 * sub, 18 + 6 * sub)
    eliminate(30, 32)
    z_sent(0)
    z_step(4, 0)
    g_arrived(1, LEFT_2, RIGHT_2)
    z_step(4, 1)
    z_step(4, 2)
    z_sent(1)
    core_arrived(1)
    for sub in range(SUBS):
        w = weights(sub)
        z_step(5, sub)
        clean_rows(sub, w, 0)
        clean_rows(sub, w, 1)
        if sub > 0:
            z_step(6, sub - 1)
        clean_rows(sub, w, 2)
        clean_rows(sub, w, 3)
    g_sent(0)
    g_sent(1)
    z_step(6, 2)
    for hop in range(2, 6):
        z_sent(hop)
    for sub in range(SUBS):
        z_step(7, sub)
        finish(sub)
    z_sent(6)
    z_sent(7)


def per_device(array_volts, reference_volts):
    volts = array_volts.reshape(SUBS, PAIR, SAMPLES)
    refs = reference_volts.reshape(SUBS, 2 * NREF, SAMPLES // COLS)
    vmem = pl.BlockSpec(memory_space=pltpu.VMEM)
    return pl.pallas_call(
        kernel,
        out_shape=jax.ShapeDtypeStruct((SUBS, 2, COLS * ANTS, ROWS * ANTS), F32),
        in_specs=[vmem, vmem],
        out_specs=vmem,
        scratch_shapes=[
            pltpu.VMEM((SUBS, ROWS, PAIR, SAMPLES), BF16),
            pltpu.VMEM((SUBS, COLS, PAIR, SAMPLES), BF16),
            pltpu.VMEM((COLS, SUBS, 2 * NREF, SAMPLES // COLS), BF16),
            pltpu.VMEM((SUBS, 2 * NREF, SAMPLES), BF16),
            pltpu.VMEM((SUBS, 2, 6 * NREF, SAMPLES), BF16),
            pltpu.VMEM((SUBS, 2 * COLS * ANTS, SAMPLES), BF16),
            pltpu.VMEM((SUBS, 2 * COLS * ANTS, SAMPLES), BF16),
            pltpu.VMEM((2, SUBS, NREF, NREF), F32),
            pltpu.SemaphoreType.DMA((2, 8, SUBS)),
            pltpu.SemaphoreType.DMA((2, 8, SUBS)),
            pltpu.SemaphoreType.DMA((2, 7)),
            pltpu.SemaphoreType.DMA((2, 7)),
            pltpu.SemaphoreType.DMA((2, 8)),
            pltpu.SemaphoreType.DMA((2, 8)),
        ],
        compiler_params=pltpu.CompilerParams(
            collective_id=0, has_side_effects=True, vmem_limit_bytes=48 * 1024 * 1024
        ),
    )(volts, refs)


def solution(mesh):
    return jax.shard_map(
        per_device,
        mesh=mesh,
        in_specs=(P("chan", None, ("row", "col"), None), P("chan", None, None, "col")),
        out_specs=P("chan", None, "row", "col"),
        check_vma=False,
    )
```

time: 239 us -> 58.2 us (0.24)
  waiting for transfers between devices: 116 us -> 0 us
  Pallas kernels: 0 us -> 55.6 us
  starting transfers between devices: 41.5 us -> 0 us
  other arithmetic: 39.4 us -> 0 us
  between operations: 13.7 us -> 0.01 us
  local copies, waits for them, and re-layouts: 14.8 us -> 2.47 us
  matrix products: 12.3 us -> 0 us
    all_gather x3 -> x0, waiting for transfers between devices: 83 us -> none  [per_device(): lax.all_gather(local_volts, 'row', axis=1, tiled=True)]
    pallas_call x0 -> x1, Pallas kernels: none -> 55.6 us  [per_device(): pl.pallas_call(kernel, out_shape=jax.ShapeDtypeStruct((SUBS, 2, COLS * AN...]
    all_to_all x6 -> x0, starting transfers between devices: 41.5 us -> none  [sent_to_all(): return lax.all_to_all(copies, axis, split_axis=0, concat_axis=0, tiled=True)]
    another operation x27 -> x0, other arithmetic: 37.5 us -> none  [the longest x9 19.7 us: subtract(): lower_factor = jnp.linalg.cholesky(system)]
    all_to_all x6 -> x0, waiting for transfers between devices: 31.3 us -> none  [sent_to_all(): return lax.all_to_all(copies, axis, split_axis=0, concat_axis=0, tiled=True)]
    dot_general x21 -> x0, matrix products: 11.1 us -> none  [the longest x9 7.68 us: correlate(): jnp.einsum('xn,yn->xy', stacked_first, stacked_second, preferred_element_...]
    broadcast_in_dim x6 -> x0, local copies, waits for them, and re-layouts: 5.59 us -> none  [sent_to_all(): copies = jnp.broadcast_to(x, (lax.axis_size(axis), *x.shape))]
  transfers between devices with their start and end apart: 9 -> 0, of which waited for: 6 -> 0; matrix products, arithmetic and copies ran while one was open for 24% -> 0% of each run, Pallas kernels for 0% -> 0%
where the time goes in v1:
time: 58.2 us; the launch traced here: 58.1 us
  Pallas kernels  55.6 us (96%)
  local copies, waits for them, and re-layouts  2.47 us (4%)
    pallas_call x1, Pallas kernels, per_device(): pl.pallas_call(kernel, out_shape=jax.ShapeDtypeStruct((SUBS, 2, COLS * AN...  55.6 us
    unnamed x5, local copies, waits for them, and re-layouts  2.47 us

profile of v1, /device:TPU:6, one launch (start us, length us, event | category | flops | bytes accessed | tf_op | source)
XLA Modules:
  0.0 58.1 jit_solution(13776724390418238304)
XLA Ops:
  0.0 0.0 copy-start
  0.0 0.9 %copy-done = bf16[3,2,8,2048]{3,2,1,0:T(8,128)(2,1)S(1)} copy-done((bf16[3,2,8,2048]{3,2,1,0:T(8,128)(2,1)S(1)}, bf16[3,2,8,2048]{3,2,1,0:T(8,128)(2,1)}, u32[]{:S(2)}) %copy-start) | copy-done | bytes 196632
  0.9 0.0 copy-start.1
  0.9 0.8 %copy-done.1 = bf16[3,2,32,128]{3,2,1,0:T(8,128)(2,1)S(1)} copy-done((bf16[3,2,32,128]{3,2,1,0:T(8,128)(2,1)S(1)}, bf16[3,2,32,128]{3,2,1,0:T(8,128)(2,1)}, u32[]{:S(2)}) %copy-start.1) | copy-done | bytes 49176
  1.7 55.6 %shard_map.28 = f32[3,2,128,128]{3,2,1,0:T(8,128)S(1)} custom-call(bf16[3,16,2048]{2,1,0:T(8,128)(2,1)S(1)} %bitcast.2, bf16[3,64,128]{2,1,0:T(8,128)(2,1)S(1)} %bitcast.3), custom_call_target="tpu_custom_call" | custom-call | tf_op jit(solution)/shard_map/pallas_call | solution.py:282
  57.3 0.7 %copy.4 = f32[3,2,128,128]{3,2,1,0:T(8,128)} copy(f32[3,2,128,128]{3,2,1,0:T(8,128)S(1)} %shard_map.28) | data formatting | bytes 786432
Async XLA Ops:
  0.0 0.9 %copy-start = (bf16[3,2,8,2048]{3,2,1,0:T(8,128)(2,1)S(1)}, bf16[3,2,8,2048]{3,2,1,0:T(8,128)(2,1)}, u32[]{:S(2)}) copy-start(bf16[3,2,8,2048]{3,2,1,0:T(8,128)(2,1)} %param.2) | copy-start | bytes 589828
  0.9 0.8 %copy-start.1 = (bf16[3,2,32,128]{3,2,1,0:T(8,128)(2,1)S(1)}, bf16[3,2,32,128]{3,2,1,0:T(8,128)(2,1)}, u32[]{:S(2)}) copy-start(bf16[3,2,32,128]{3,2,1,0:T(8,128)(2,1)} %param.3) | copy-start | bytes 147460

commit v2 on v1

--- a/solution.py
+++ b/solution.py
@@ -41,14 +41,17 @@
         pl.semaphore_signal(barrier, inc=1, device_id={axis: there}, device_id_type=MESH)
     pl.semaphore_wait(barrier, 6)
 
-    def hops(way, sub):
-        return 8 if (sub % 2) == way else 7
-
-    def z_copy(way, hop, sub):
-        start = lax.rem(row + (ROWS - hop if way == 0 else hop), ROWS)
-        place = colb.at[sub, start]
+    def reach(way, start, sub):
+        up_hops = 7 + jnp.asarray(sub != 1).astype(jnp.int32)
+        return up_hops if way == 0 else ROWS - 1 - up_hops
+
+    def z_start(way, hop, sub):
+        return lax.rem(row + (ROWS - hop if way == 0 else hop), ROWS)
+
+    def z_copy(way, hop, sub, mine=False):
+        place = colb.at[sub, z_start(way, hop, sub)]
         return pltpu.make_async_remote_copy(
-            src_ref=volts.at[sub] if hop == 0 else place,
+            src_ref=volts.at[sub] if mine else place,
             dst_ref=place,
             send_sem=z_send.at[way, hop, sub],
             recv_sem=z_recv.at[way, hop, sub],
@@ -56,18 +59,39 @@
             device_id_type=MESH,
         )
 
-    def z_step(hop, sub):
-        for way in range(2):
-            if hop < hops(way, sub):
-                z_copy(way, hop, sub).wait_recv()
-                if hop + 1 < hops(way, sub):
-                    z_copy(way, hop + 1, sub).start()
+    def z_event(way, n):
+        hop, sub = n // SUBS, lax.rem(n, SUBS)
+        hops = reach(way, z_start(way, hop + 1, sub), sub)
+
+        @pl.when(hop + 1 <= hops)
+        def _():
+            z_copy(way, hop, sub).wait_recv()
+
+        @pl.when(hop + 2 <= hops)
+        def _():
+            z_copy(way, hop + 1, sub).start()
+
+    def z_step(n):
+        z_event(0, n)
+        z_event(1, n)
+
+    def z_steps(first, last, job):
+        def body(n, carry):
+            z_step(n)
+            job(n - first)
+            return carry
+
+        lax.fori_loop(first, last, body, jnp.int32(0))
 
     def z_sent(hop):
-        for way in range(2):
-            for sub in range(SUBS):
-                if hop < hops(way, sub):
-                    z_copy(way, hop, sub).wait_send()
+        for sub in range(SUBS):
+            for way in range(2):
+                if hop == 0:
+                    z_copy(way, hop, sub, True).wait_send()
+                else:
+                    @pl.when(hop + 1 <= reach(way, z_start(way, hop, sub), sub))
+                    def _():
+                        z_copy(way, hop, sub).wait_send()
 
     def shard(kind, slot):
         return refb.at[slot] if kind == 0 else rowb.at[:, slot]
@@ -211,7 +235,7 @@
 
     for sub in range(SUBS):
         for way in range(2):
-            z_copy(way, 0, sub).start()
+            z_copy(way, 0, sub, True).start()
         if sub == 0:
             g_start(0)
     g_start(1)
@@ -220,59 +244,60 @@
         rowb[sub, col] = volts[sub]
     refb[col] = refs[...]
 
-    z_step(0, 0)
-    g_arrived(0, FROM_Y, LEFT, RIGHT)
-    g_forward(0, LEFT_Y, RIGHT_Y, LEFT_2)
-    z_step(0, 1)
-    z_step(0, 2)
-    g_arrived(0, LEFT_Y, RIGHT_Y, LEFT_2)
-    g_forward(0, RIGHT_2)
-    z_step(1, 0)
-    g_arrived(1, FROM_Y, LEFT, RIGHT)
-    g_forward(1, LEFT_Y, RIGHT_Y, LEFT_2)
-    g_arrived(0, RIGHT_2)
-    z_step(1, 1)
-    z_step(1, 2)
-    core_arrived(0)
-    gather_references()
-    z_step(2, 0)
-    covariance()
-    z_step(2, 1)
-    eliminate(0, 6)
-    z_step(2, 2)
-    g_arrived(1, LEFT_Y, RIGHT_Y)
-    g_forward(1, RIGHT_2)
-    eliminate(6, 12)
-    for sub in range(SUBS):
-        z_step(3, sub)
-        eliminate(12 + 6 * sub, 18 + 6 * sub)
-    eliminate(30, 32)
-    z_sent(0)
-    z_step(4, 0)
-    g_arrived(1, LEFT_2, RIGHT_2)
-    z_step(4, 1)
-    z_step(4, 2)
-    z_sent(1)
+    def rows_first():
+        g_arrived(1, FROM_Y, LEFT, RIGHT)
+        g_forward(1, LEFT_Y, RIGHT_Y, LEFT_2)
+
+    def rows_second():
+        g_arrived(1, LEFT_Y, RIGHT_Y)
+        g_forward(1, RIGHT_2)
+
+    def refs_first():
+        g_arrived(0, FROM_Y, LEFT, RIGHT)
+        g_forward(0, LEFT_Y, RIGHT_Y, LEFT_2)
+
+    def refs_second():
+        g_arrived(0, LEFT_Y, RIGHT_Y, LEFT_2)
+        g_forward(0, RIGHT_2)
+
+    def refs_here():
+        core_arrived(0)
+        gather_references()
+
+    def rows_done():
+        g_arrived(1, LEFT_2, RIGHT_2)
+
+    def eliminate_four(n):
+        eliminate(4 * n, 4 * n + 4)
+
+    def rows_cleaned(sub):
+        w = weights(sub)
+        for part in range(SAMPLES // LANES):
+            clean_rows(sub, w, part)
+
+    after = {
+        1: refs_first, 3: refs_second, 4: rows_first, 5: functools.partial(g_arrived, 0, RIGHT_2),
+        6: refs_here, 7: covariance,
+    }
+    for n in range(8):
+        z_step(jnp.int32(n))
+        if n in after:
+            after[n]()
+    z_steps(8, 12, eliminate_four)
+    rows_second()
+    z_steps(12, 16, lambda n: eliminate_four(n + 4))
+    rows_done()
+    z_step(jnp.int32(16))
     core_arrived(1)
-    for sub in range(SUBS):
-        w = weights(sub)
-        z_step(5, sub)
-        clean_rows(sub, w, 0)
-        clean_rows(sub, w, 1)
-        if sub > 0:
-            z_step(6, sub - 1)
-        clean_rows(sub, w, 2)
-        clean_rows(sub, w, 3)
+    z_steps(17, 20, rows_cleaned)
+    z_step(jnp.int32(20))
+    for hop in range(6):
+        z_sent(hop)
     g_sent(0)
     g_sent(1)
-    z_step(6, 2)
-    for hop in range(2, 6):
+    z_steps(21, 24, finish)
+    for hop in range(6, 8):
         z_sent(hop)
-    for sub in range(SUBS):
-        z_step(7, sub)
-        finish(sub)
-    z_sent(6)
-    z_sent(7)
 
 
 def per_device(array_volts, reference_volts):

time: 58.2 us -> 54.8 us (0.942)
  Pallas kernels: 55.6 us -> 52.1 us
    pallas_call x1, Pallas kernels: 55.6 us -> 52.1 us  [per_device(): pl.pallas_call(kernel, out_shape=jax.ShapeDtypeStruct((SUBS, 2, COLS * AN...]
where the time goes in v2:
time: 54.8 us; the launch traced here: 54.6 us
  Pallas kernels  52.1 us (95%)
  local copies, waits for them, and re-layouts  2.47 us (5%)
    pallas_call x1, Pallas kernels, per_device(): pl.pallas_call(kernel, out_shape=jax.ShapeDtypeStruct((SUBS, 2, COLS * AN...  52.1 us
    unnamed x5, local copies, waits for them, and re-layouts  2.47 us

profile of v2, /device:TPU:6, one launch (start us, length us, event | category | flops | bytes accessed | tf_op | source)
XLA Modules:
  0.0 54.6 jit_solution(1572490694312100328)
XLA Ops:
  0.0 0.0 copy-start
  0.0 0.9 %copy-done = bf16[3,2,8,2048]{3,2,1,0:T(8,128)(2,1)S(1)} copy-done((bf16[3,2,8,2048]{3,2,1,0:T(8,128)(2,1)S(1)}, bf16[3,2,8,2048]{3,2,1,0:T(8,128)(2,1)}, u32[]{:S(2)}) %copy-start) | copy-done | bytes 196632
  0.9 0.0 copy-start.1
  0.9 0.8 %copy-done.1 = bf16[3,2,32,128]{3,2,1,0:T(8,128)(2,1)S(1)} copy-done((bf16[3,2,32,128]{3,2,1,0:T(8,128)(2,1)S(1)}, bf16[3,2,32,128]{3,2,1,0:T(8,128)(2,1)}, u32[]{:S(2)}) %copy-start.1) | copy-done | bytes 49176
  1.7 52.1 %shard_map.28 = f32[3,2,128,128]{3,2,1,0:T(8,128)S(1)} custom-call(bf16[3,16,2048]{2,1,0:T(8,128)(2,1)S(1)} %bitcast.2, bf16[3,64,128]{2,1,0:T(8,128)(2,1)S(1)} %bitcast.3), custom_call_target="tpu_custom_call" | custom-call | tf_op jit(solution)/shard_map/pallas_call | solution.py:307
  53.8 0.7 %copy.4 = f32[3,2,128,128]{3,2,1,0:T(8,128)} copy(f32[3,2,128,128]{3,2,1,0:T(8,128)S(1)} %shard_map.28) | data formatting | bytes 786432
Async XLA Ops:
  0.0 0.9 %copy-start = (bf16[3,2,8,2048]{3,2,1,0:T(8,128)(2,1)S(1)}, bf16[3,2,8,2048]{3,2,1,0:T(8,128)(2,1)}, u32[]{:S(2)}) copy-start(bf16[3,2,8,2048]{3,2,1,0:T(8,128)(2,1)} %param.2) | copy-start | bytes 589828
  0.9 0.8 %copy-start.1 = (bf16[3,2,32,128]{3,2,1,0:T(8,128)(2,1)S(1)}, bf16[3,2,32,128]{3,2,1,0:T(8,128)(2,1)}, u32[]{:S(2)}) copy-start(bf16[3,2,32,128]{3,2,1,0:T(8,128)(2,1)} %param.3) | copy-start | bytes 147460

commit v3 on v2

--- a/solution.py
+++ b/solution.py
@@ -18,7 +18,7 @@
 
 
 def kernel(volts, refs, out, colb, rowb, refb, ref_all, ref_mix, hi, lo, inv, *sems):
-    z_send, z_recv, g_send, g_recv, c_send, c_recv = sems
+    z_send, z_recv, g_send, g_recv, c_send, c_recv, own_sem = sems
     row, col = lax.axis_index("row"), lax.axis_index("col")
     up, down = lax.rem(row + 1, ROWS), lax.rem(row + ROWS - 1, ROWS)
     y, x, core = col // (2 * NX), lax.rem(col // 2, NX), lax.rem(col, 2)
@@ -239,10 +239,13 @@
         if sub == 0:
             g_start(0)
     g_start(1)
-    for sub in range(SUBS):
-        colb[sub, row] = volts[sub]
-        rowb[sub, col] = volts[sub]
-    refb[col] = refs[...]
+    own = [
+        pltpu.make_async_copy(volts, colb.at[:, row], own_sem.at[0]),
+        pltpu.make_async_copy(volts, rowb.at[:, col], own_sem.at[1]),
+        pltpu.make_async_copy(refs, refb.at[col], own_sem.at[2]),
+    ]
+    for copy in own:
+        copy.start()
 
     def rows_first():
         g_arrived(1, FROM_Y, LEFT, RIGHT)
@@ -281,6 +284,9 @@
     }
     for n in range(8):
         z_step(jnp.int32(n))
+        if n == 2:
+            for copy in own:
+                copy.wait()
         if n in after:
             after[n]()
     z_steps(8, 12, eliminate_four)
@@ -304,10 +310,13 @@
     volts = array_volts.reshape(SUBS, PAIR, SAMPLES)
     refs = reference_volts.reshape(SUBS, 2 * NREF, SAMPLES // COLS)
     vmem = pl.BlockSpec(memory_space=pltpu.VMEM)
+    hbm = pl.BlockSpec(memory_space=pltpu.HBM)
+    volts = pltpu.with_memory_space_constraint(volts, pltpu.HBM)
+    refs = pltpu.with_memory_space_constraint(refs, pltpu.HBM)
     return pl.pallas_call(
         kernel,
         out_shape=jax.ShapeDtypeStruct((SUBS, 2, COLS * ANTS, ROWS * ANTS), F32),
-        in_specs=[vmem, vmem],
+        in_specs=[hbm, hbm],
         out_specs=vmem,
         scratch_shapes=[
             pltpu.VMEM((SUBS, ROWS, PAIR, SAMPLES), BF16),
@@ -324,6 +333,7 @@
             pltpu.SemaphoreType.DMA((2, 7)),
             pltpu.SemaphoreType.DMA((2, 8)),
             pltpu.SemaphoreType.DMA((2, 8)),
+            pltpu.SemaphoreType.DMA((3,)),
         ],
         compiler_params=pltpu.CompilerParams(
             collective_id=0, has_side_effects=True, vmem_limit_bytes=48 * 1024 * 1024

time: 54.8 us -> 53.2 us (0.971)
  local copies, waits for them, and re-layouts: 2.47 us -> 0.75 us
    unnamed x5 -> x1, local copies, waits for them, and re-layouts: 2.47 us -> 0.75 us
where the time goes in v3:
time: 53.2 us; the launch traced here: 53.1 us
  Pallas kernels  52.3 us (98%)
  local copies, waits for them, and re-layouts  0.75 us (1%)
    pallas_call x1, Pallas kernels, per_device(): pl.pallas_call(kernel, out_shape=jax.ShapeDtypeStruct((SUBS, 2, COLS * AN...  52.3 us

profile of v3, /device:TPU:6, one launch (start us, length us, event | category | flops | bytes accessed | tf_op | source)
XLA Modules:
  0.0 53.1 jit_solution(9594264814409581789)
XLA Ops:
  0.0 52.3 %shard_map.28 = f32[3,2,128,128]{3,2,1,0:T(8,128)S(1)} custom-call(bf16[3,16,2048]{2,1,0:T(8,128)(2,1)} %bitcast.2, bf16[3,64,128]{2,1,0:T(8,128)(2,1)} %bitcast.3), custom_call_target="tpu_custom_call" | custom-call | tf_op jit(solution)/shard_map/pallas_call | solution.py:316
  52.3 0.7 %copy.4 = f32[3,2,128,128]{3,2,1,0:T(8,128)} copy(f32[3,2,128,128]{3,2,1,0:T(8,128)S(1)} %shard_map.28) | data formatting | bytes 786432

commit v4 on v3

--- a/solution.py
+++ b/solution.py
@@ -43,6 +43,8 @@
 
     def reach(way, start, sub):
         up_hops = 7 + jnp.asarray(sub != 1).astype(jnp.int32)
+        up_hops = jnp.where(start == 8, 7, up_hops)
+        up_hops = jnp.where(start == 9, 7, up_hops)
         return up_hops if way == 0 else ROWS - 1 - up_hops
 
     def z_start(way, hop, sub):
@@ -181,12 +183,9 @@
             col_im = jnp.sum(jnp.where(on_lane, im, 0.0), axis=2, keepdims=True)
             row_re = jnp.sum(jnp.where(on_line, re, 0.0), axis=1, keepdims=True)
             row_im = jnp.sum(jnp.where(on_line, im, 0.0), axis=1, keepdims=True)
-            both = jnp.logical_and(on_lane, on_line)
-            pivot = jnp.sum(
-                jnp.sum(jnp.where(both, re, 0.0), axis=2, keepdims=True), axis=1, keepdims=True
-            )
+            first_lane = lax.broadcasted_iota(jnp.int32, (SUBS, 1, NREF), 2) == k
+            pivot = jnp.sum(jnp.where(first_lane, row_re, 0.0), axis=2, keepdims=True)
             scale = 1.0 / pivot
-            first_lane = lax.broadcasted_iota(jnp.int32, (SUBS, 1, NREF), 2) == k
             row_re = jnp.where(first_lane, 1.0, row_re) * scale
             row_im = jnp.where(first_lane, 0.0, row_im) * scale
             new_re = jnp.where(on_lane, 0.0, re) - (col_re * row_re - col_im * row_im)
@@ -267,11 +266,8 @@
         core_arrived(0)
         gather_references()
 
-    def rows_done():
-        g_arrived(1, LEFT_2, RIGHT_2)
-
-    def eliminate_four(n):
-        eliminate(4 * n, 4 * n + 4)
+    def eliminate_some(n):
+        eliminate(5 * n, jnp.minimum(5 * n + 5, NREF))
 
     def rows_cleaned(sub):
         w = weights(sub)
@@ -279,23 +275,28 @@
             clean_rows(sub, w, part)
 
     after = {
-        1: refs_first, 3: refs_second, 4: rows_first, 5: functools.partial(g_arrived, 0, RIGHT_2),
-        6: refs_here, 7: covariance,
+        1: [refs_first], 3: [refs_second], 4: [rows_first], 5: [functools.partial(g_arrived, 0, RIGHT_2)],
+        6: [refs_here], 7: [covariance],
     }
     for n in range(8):
         z_step(jnp.int32(n))
         if n == 2:
             for copy in own:
                 copy.wait()
-        if n in after:
-            after[n]()
-    z_steps(8, 12, eliminate_four)
-    rows_second()
-    z_steps(12, 16, lambda n: eliminate_four(n + 4))
-    rows_done()
-    z_step(jnp.int32(16))
+        for job in after.get(n, ()):
+            job()
+    z_steps(8, 9, eliminate_some)
+    g_arrived(1, RIGHT_Y)
+    g_forward(1, RIGHT_2)
+    z_steps(9, 12, lambda n: eliminate_some(n + 1))
+    g_arrived(1, LEFT_Y, LEFT_2)
+    z_steps(12, 14, lambda n: eliminate_some(n + 4))
+    g_arrived(1, RIGHT_2)
+    z_steps(14, 15, lambda n: eliminate_some(n + 6))
     core_arrived(1)
-    z_steps(17, 20, rows_cleaned)
+    z_steps(15, 18, rows_cleaned)
+    z_step(jnp.int32(18))
+    z_step(jnp.int32(19))
     z_step(jnp.int32(20))
     for hop in range(6):
         z_sent(hop)
@@ -327,8 +328,8 @@
             pltpu.VMEM((SUBS, 2 * COLS * ANTS, SAMPLES), BF16),
             pltpu.VMEM((SUBS, 2 * COLS * ANTS, SAMPLES), BF16),
             pltpu.VMEM((2, SUBS, NREF, NREF), F32),
-            pltpu.SemaphoreType.DMA((2, 8, SUBS)),
-            pltpu.SemaphoreType.DMA((2, 8, SUBS)),
+            pltpu.SemaphoreType.DMA((2, 9, SUBS)),
+            pltpu.SemaphoreType.DMA((2, 9, SUBS)),
             pltpu.SemaphoreType.DMA((2, 7)),
             pltpu.SemaphoreType.DMA((2, 7)),
             pltpu.SemaphoreType.DMA((2, 8)),

time: 53.2 us -> 52 us (0.977)
  Pallas kernels: 52.3 us -> 51.2 us
    pallas_call x1, Pallas kernels: 52.3 us -> 51.2 us  [per_device(): pl.pallas_call(kernel, out_shape=jax.ShapeDtypeStruct((SUBS, 2, COLS * AN...]
where the time goes in v4:
time: 52 us; the launch traced here: 51.9 us
  Pallas kernels  51.2 us (98%)
  local copies, waits for them, and re-layouts  0.75 us (1%)
    pallas_call x1, Pallas kernels, per_device(): pl.pallas_call(kernel, out_shape=jax.ShapeDtypeStruct((SUBS, 2, COLS * AN...  51.2 us

profile of v4, /device:TPU:6, one launch (start us, length us, event | category | flops | bytes accessed | tf_op | source)
XLA Modules:
  0.0 51.9 jit_solution(15580882788938539272)
XLA Ops:
  0.0 51.2 %shard_map.28 = f32[3,2,128,128]{3,2,1,0:T(8,128)S(1)} custom-call(bf16[3,16,2048]{2,1,0:T(8,128)(2,1)} %bitcast.2, bf16[3,64,128]{2,1,0:T(8,128)(2,1)} %bitcast.3), custom_call_target="tpu_custom_call" | custom-call | tf_op jit(solution)/shard_map/pallas_call | solution.py:317
  51.2 0.7 %copy.4 = f32[3,2,128,128]{3,2,1,0:T(8,128)} copy(f32[3,2,128,128]{3,2,1,0:T(8,128)S(1)} %shard_map.28) | data formatting | bytes 786432

commit v5 on v4

--- a/solution.py
+++ b/solution.py
@@ -45,6 +45,8 @@
         up_hops = 7 + jnp.asarray(sub != 1).astype(jnp.int32)
         up_hops = jnp.where(start == 8, 7, up_hops)
         up_hops = jnp.where(start == 9, 7, up_hops)
+        up_hops = jnp.where(start == 10, 7, up_hops)
+        up_hops = jnp.where(start == 11, 7, up_hops)
         return up_hops if way == 0 else ROWS - 1 - up_hops
 
     def z_start(way, hop, sub):
@@ -296,14 +298,17 @@
     core_arrived(1)
     z_steps(15, 18, rows_cleaned)
     z_step(jnp.int32(18))
+    z_sent(0)
+    z_sent(1)
+    g_sent(0)
     z_step(jnp.int32(19))
+    z_sent(2)
+    z_sent(3)
+    g_sent(1)
     z_step(jnp.int32(20))
-    for hop in range(6):
-        z_sent(hop)
-    g_sent(0)
-    g_sent(1)
+    z_sent(4)
     z_steps(21, 24, finish)
-    for hop in range(6, 8):
+    for hop in range(5, 8):
         z_sent(hop)
 
 

time: 52 us -> 52.1 us (level)
  no operation moved by 1% of the time
where the time goes in v5:
time: 52.1 us; the launch traced here: 52 us
  Pallas kernels  51.2 us (98%)
  local copies, waits for them, and re-layouts  0.75 us (1%)
    pallas_call x1, Pallas kernels, per_device(): pl.pallas_call(kernel, out_shape=jax.ShapeDtypeStruct((SUBS, 2, COLS * AN...  51.2 us

profile of v5, /device:TPU:6, one launch (start us, length us, event | category | flops | bytes accessed | tf_op | source)
XLA Modules:
  0.0 52.0 jit_solution(17009709138010292546)
XLA Ops:
  0.0 51.2 %shard_map.28 = f32[3,2,128,128]{3,2,1,0:T(8,128)S(1)} custom-call(bf16[3,16,2048]{2,1,0:T(8,128)(2,1)} %bitcast.2, bf16[3,64,128]{2,1,0:T(8,128)(2,1)} %bitcast.3), custom_call_target="tpu_custom_call" | custom-call | tf_op jit(solution)/shard_map/pallas_call | solution.py:322
  51.2 0.7 %copy.4 = f32[3,2,128,128]{3,2,1,0:T(8,128)} copy(f32[3,2,128,128]{3,2,1,0:T(8,128)S(1)} %shard_map.28) | data formatting | bytes 786432

commit v6 on v4

--- a/solution.py
+++ b/solution.py
@@ -17,7 +17,7 @@
 FROM_Y, LEFT, RIGHT, LEFT_Y, RIGHT_Y, LEFT_2, RIGHT_2, OWN = range(8)
 
 
-def kernel(volts, refs, out, colb, rowb, refb, ref_all, ref_mix, hi, lo, inv, *sems):
+def kernel(volts, refs, out, colb, rowb, refb, ref_all, ref_mix, hi, lo, inv, w_now, *sems):
     z_send, z_recv, g_send, g_recv, c_send, c_recv, own_sem = sems
     row, col = lax.axis_index("row"), lax.axis_index("col")
     up, down = lax.rem(row + 1, ROWS), lax.rem(row + ROWS - 1, ROWS)
@@ -45,6 +45,8 @@
         up_hops = 7 + jnp.asarray(sub != 1).astype(jnp.int32)
         up_hops = jnp.where(start == 8, 7, up_hops)
         up_hops = jnp.where(start == 9, 7, up_hops)
+        up_hops = jnp.where(start == 10, 7, up_hops)
+        up_hops = jnp.where(start == 11, 7, up_hops)
         return up_hops if way == 0 else ROWS - 1 - up_hops
 
     def z_start(way, hop, sub):
@@ -268,11 +270,6 @@
 
     def eliminate_some(n):
         eliminate(5 * n, jnp.minimum(5 * n + 5, NREF))
-
-    def rows_cleaned(sub):
-        w = weights(sub)
-        for part in range(SAMPLES // LANES):
-            clean_rows(sub, w, part)
 
     after = {
         1: [refs_first], 3: [refs_second], 4: [rows_first], 5: [functools.partial(g_arrived, 0, RIGHT_2)],
@@ -294,16 +291,25 @@
     g_arrived(1, RIGHT_2)
     z_steps(14, 15, lambda n: eliminate_some(n + 6))
     core_arrived(1)
-    z_steps(15, 18, rows_cleaned)
-    z_step(jnp.int32(18))
-    z_step(jnp.int32(19))
-    z_step(jnp.int32(20))
-    for hop in range(6):
+    def rows_part(n):
+        sub = n // 2
+
+        @pl.when(lax.rem(n, 2) == 0)
+        def _():
+            w_now[...] = weights(sub)
+
+        @pl.when(lax.rem(n, 2) == 1)
+        def _():
+            for part in range(SAMPLES // LANES):
+                clean_rows(sub, w_now[...], part)
+
+    z_steps(15, 21, rows_part)
+    for hop in range(5):
         z_sent(hop)
     g_sent(0)
     g_sent(1)
     z_steps(21, 24, finish)
-    for hop in range(6, 8):
+    for hop in range(5, 8):
         z_sent(hop)
 
 
@@ -328,6 +334,7 @@
             pltpu.VMEM((SUBS, 2 * COLS * ANTS, SAMPLES), BF16),
             pltpu.VMEM((SUBS, 2 * COLS * ANTS, SAMPLES), BF16),
             pltpu.VMEM((2, SUBS, NREF, NREF), F32),
+            pltpu.VMEM((COLS * ANTS, 6 * NREF), BF16),
             pltpu.SemaphoreType.DMA((2, 9, SUBS)),
             pltpu.SemaphoreType.DMA((2, 9, SUBS)),
             pltpu.SemaphoreType.DMA((2, 7)),

time: 52 us -> 51.6 us (level)
  Pallas kernels: 51.2 us -> 50.5 us
    pallas_call x1, Pallas kernels: 51.2 us -> 50.5 us  [per_device(): pl.pallas_call(kernel, out_shape=jax.ShapeDtypeStruct((SUBS, 2, COLS * AN...]
where the time goes in v6:
time: 51.6 us; the launch traced here: 51.3 us
  Pallas kernels  50.5 us (98%)
  local copies, waits for them, and re-layouts  0.75 us (1%)
    pallas_call x1, Pallas kernels, per_device(): pl.pallas_call(kernel, out_shape=jax.ShapeDtypeStruct((SUBS, 2, COLS * AN...  50.5 us

profile of v6, /device:TPU:6, one launch (start us, length us, event | category | flops | bytes accessed | tf_op | source)
XLA Modules:
  0.0 51.3 jit_solution(8888724789884226678)
XLA Ops:
  0.0 50.5 %shard_map.28 = f32[3,2,128,128]{3,2,1,0:T(8,128)S(1)} custom-call(bf16[3,16,2048]{2,1,0:T(8,128)(2,1)} %bitcast.2, bf16[3,64,128]{2,1,0:T(8,128)(2,1)} %bitcast.3), custom_call_target="tpu_custom_call" | custom-call | tf_op jit(solution)/shard_map/pallas_call | solution.py:323
  50.5 0.7 %copy.4 = f32[3,2,128,128]{3,2,1,0:T(8,128)} copy(f32[3,2,128,128]{3,2,1,0:T(8,128)S(1)} %shard_map.28) | data formatting | bytes 786432
